TPU v7x, 32 devices: a whole 2x2x4 slice. The times are simulated.
32 devices in a mesh: wide: 2 (over core), narrow: 16 (over z, y, x).
Axes of the slice: x: 2, y: 2, z: 4, core: 2. Of those that a mesh axis runs over, the one named last changes fastest.
Arguments:
- tokens: bfloat16 [16384, 1024], P(('wide', 'narrow')), may hold values from -6 to 6
- cotangent: bfloat16 [16384, 1024], P(('wide', 'narrow')), may hold values from -6 to 6
- loss_mask: int32 [16384], P(('wide', 'narrow')), may hold values 0 or 1
- seq_lengths: int32 [32, 3], P(('wide', 'narrow')), may hold values from 1 to 384, 512 in all within a row
- norm_gain: float32 [1024], P('narrow'), may hold values from 0.5 to 1.5
- in_proj: float32 [1024, 4096], P('narrow'), may hold values from -0.1875 to 0.1875
- conv_weight: float32 [4, 2048], P(None, 'narrow'), may hold values from -3 to 3
- conv_bias: float32 [2048], P('narrow'), may hold values from -3 to 3
- select_proj: float32 [96, 2048], P(None, 'narrow'), may hold values from -0.125 to 0.125
- step_proj: float32 [64, 2048], P(None, 'narrow'), may hold values from -0.75 to 0.75
- step_bias: float32 [2048], P('narrow'), may hold values from -5 to -2
- decay_log: float32 [16, 2048], P(None, 'narrow'), may hold values from 0 to 2.8
- skip_scale: float32 [2048], P('narrow'), may hold values from 0.5 to 1.5
- out_proj: float32 [2048, 1024], P('narrow'), may hold values from -0.125 to 0.125
Outputs:
- output: bfloat16 [16384, 1024], P(('wide', 'narrow'))
- grad_tokens: bfloat16 [16384, 1024], P(('wide', 'narrow'))
- grad_norm_gain: float32 [1024], P('narrow')
- grad_in_proj: float32 [1024, 4096], P('narrow')
- grad_conv_weight: float32 [4, 2048], P(None, 'narrow')
- grad_conv_bias: float32 [2048], P('narrow')
- grad_select_proj: float32 [96, 2048], P(None, 'narrow')
- grad_step_proj: float32 [64, 2048], P(None, 'narrow')
- grad_step_bias: float32 [2048], P('narrow')
- grad_decay_log: float32 [16, 2048], P(None, 'narrow')
- grad_skip_scale: float32 [2048], P('narrow')
- grad_out_proj: float32 [2048, 1024], P('narrow')
- decay_sq: float32 [], replicated
- plain_sq: float32 [], replicated
Inputs may be any that keep to these rules, and one draw needn't show every extreme that they name: `seq_lengths`: each row holds 3 lengths that sum to 512; the longest of each row is exactly 384.
All inputs are finite; a program needn't handle non-finite values. No bound on the sum of `loss_mask` on one device may be relied on, other than what follows from the above.
Results may differ from a plain program's by a relative error of at most 0.0055.
The roundings to bfloat16 on the way count: a program that leaves them out, or rounds other values in their place, can miss the bound.
Values may be sent and summed in bfloat16 or wider, within the bound.
A program may use at most 192 MiB of HBM per device.

v0:
```python
import functools
import math

import jax
import jax.numpy as jnp
import numpy as np
from jax import lax
from jax.experimental import pallas as pl
from jax.experimental.pallas import tpu as pltpu
from jax.sharding import PartitionSpec as P

epsilon = 1e-05
chunk = 8
lanes = 128
log2e = math.log2(math.e)
ln2 = math.log(2.0)
far = 1e30
tiny = 1e-30


def contract(left, right, left_dim, right_dim):
    return lax.dot_general(
        left, right, (((left_dim,), (right_dim,)), ((), ())), preferred_element_type=jnp.float32
    )


def row_loop(rows, group, body, initial):
    def some(index, carry):
        return body(index, pl.ds(pl.multiple_of(index * group, group), group), carry)

    return lax.fori_loop(0, rows // group, some, initial)


def cut(tile):
    return pl.ds(tile * lanes, lanes)


def sigmoid(values):
    return 0.5 * jnp.tanh(0.5 * values) + 0.5


def softplus(values):
    small = jnp.exp(-jnp.abs(values))
    series = small * (1.0 - small * (0.5 - small * (1.0 / 3.0 - 0.25 * small)))
    return jnp.maximum(values, 0.0) + jnp.where(small < 0.03, series, jnp.log(1.0 + small))


def slope_of(step):
    return 1.0 - jnp.exp(-step)


def fill_offsets(lengths_ref, offset_buf, rows):
    place = lax.broadcasted_iota(jnp.int32, offset_buf.shape, 0)
    start = jnp.zeros(offset_buf.shape, jnp.int32)
    ahead = jnp.int32(0)
    for index in range(lengths_ref.shape[1] - 1):
        ahead = ahead + lengths_ref[0, index]
        start = jnp.where(place >= ahead, ahead, start)
    offset_buf[...] = jnp.where(place < rows, place - start, 0)


def small_rows(small_ref, first, count):
    base = first // 16 * 16
    tall = -(-(first + count - base) // 16) * 16
    return small_ref[base : base + tall, :].astype(jnp.float32)[first - base : first - base + count]


def eight(values):
    total = values[:8]
    for row in range(8, values.shape[0], 8):
        total = total + values[row : row + 8]
    return total


def conv_rows(index, at, group, tile, branch_ref, offset_buf, taps, shift):
    count = taps.shape[0]
    here = slice(tile * lanes, (tile + 1) * lanes)
    current = branch_ref[at, cut(tile)]
    before = branch_ref[pl.ds(pl.multiple_of(jnp.maximum(index * group - 8, 0), 8), 8), cut(tile)]
    both = jnp.concatenate([before, current], axis=0)
    offsets = offset_buf[at, :]
    summed = shift[:, here] + taps[count - 1 : count, here] * current
    for tap in range(count - 1):
        lag = count - 1 - tap
        read = jnp.where(offsets >= lag, pltpu.roll(both, lag, 0)[8:], 0.0)
        summed = summed + taps[tap : tap + 1, here] * read
    return summed


def rows_of(blocks):
    return as_matrix(blocks[...][None])


def as_matrix(blocks):
    columns = blocks.shape[3]
    if blocks.shape[2] % 16:
        return blocks.astype(jnp.float32).reshape(-1, columns).astype(blocks.dtype)
    return blocks.reshape(-1, columns)


def front_kernel(
    plan,
    dims,
    names,
    lengths_ref,
    tokens_ref,
    cotangent_ref,
    mask_ref,
    *refs,
):
    smalls, in_ref, out_ref, refs = refs[: len(names)], refs[len(names)], refs[len(names) + 1], refs[len(names) + 2 :]
    branch_ref, signal_ref, slope_ref, projected_ref, flipped_ref, normed_ref, low_ref = refs[:7]
    write_pair, read_pair, small_out, gain_ref, whole_ref, gate_lines, out_lines = refs[7:14]
    offset_buf, pack_buf, own_small, own_in, own_gate, own_out, land_small, land_in, store_sem = refs[14:23]
    own_gain, land_gain, gain_send, gain_recv = refs[23:27]
    rows = tokens_ref.shape[0]
    width = branch_ref.shape[1]
    block = pl.program_id(0)
    last = whole_ref.shape[0]
    shares = own_out.shape[0]
    gather = Gather(
        dims,
        [own_small] + [own_in.at[index] for index in range(last)],
        [land_small] + [land_in.at[index] for index in range(last)],
        refs[27:30],
    )
    rise = Rise(
        dims,
        [own.at[index] for index in range(shares) for own in (own_gate, own_out)],
        [lines.at[index] for index in range(shares) for lines in (gate_lines, out_lines)],
        refs[30:],
    )
    tall = pack_buf.shape[0] // 2

    def stored(index):
        return pltpu.make_async_copy(land_in.at[index], whole_ref.at[index], store_sem.at[index])

    def move_on(plan_of_moves):
        for moment, legs in plan_of_moves:

            @pl.when(block == moment)
            def _(legs=legs):
                for which, number in legs:
                    gather.leg(which, number)

    @pl.when(block == 0)
    def _():
        pack_buf[...] = jnp.zeros_like(pack_buf)
        for name, ref in zip(names, smalls):
            first, height = plan[name]
            pack_buf[first : first + height, : ref.shape[1]] = ref[...]
        own_gain[...] = jnp.zeros_like(own_gain)
        own_gain[0:1, : gain_ref.shape[1] // land_gain.shape[0]] = smalls[names.index("gain")][...]
        for side in range(2):
            own_small[side] = pack_buf[side * tall : (side + 1) * tall, :].astype(own_small.dtype)
        for index in range(last):
            own_in[index] = in_ref[:, index * width : (index + 1) * width].astype(own_in.dtype)
        place = Place(dims)
        place.greet(everyone=True)
        send_to_all(place, lambda target: own_gain, land_gain, gain_send, gain_recv)
        for index in (1, 0) + tuple(range(2, last + 1)):
            gather.start(index)
        first = last * width
        for index in range(shares):
            each = own_gate.shape[2]
            own_gate[index] = in_ref[:, first + index * each : first + (index + 1) * each].astype(own_gate.dtype)
            each = own_out.shape[2]
            own_out[index] = out_ref[:, index * each : (index + 1) * each].astype(own_out.dtype)
        for index in range(2 * shares):
            rise.start(index)
        fill_offsets(lengths_ref, offset_buf, rows)
        gather.leg(1, 1)
        gather.leg(0, 1)
        wait_for_all(place, own_gain[...], land_gain, gain_send, gain_recv)
        each = gain_ref.shape[1] // land_gain.shape[0]
        for owner in range(land_gain.shape[0]):
            gain_ref[:, owner * each : (owner + 1) * each] = (
                land_gain[owner, 0:1, :each].astype(jnp.bfloat16).astype(jnp.float32)
            )

        def norm(index, at, carry):
            residual = tokens_ref[at, :].astype(jnp.float32)
            scale = lax.rsqrt(jnp.mean(residual * residual, axis=1, keepdims=True) + epsilon)
            normed_ref[at, :] = (residual * scale * gain_ref[...]).astype(normed_ref.dtype)
            return carry

        row_loop(rows, 16, norm, 0)
        gather.leg(1, 2)
        gather.leg(0, 2)
        gather.leg(2, 1)
        flipped_ref[...] = normed_ref[...].T
        gather.leg(1, 3)
        gather.leg(0, 3)
        gather.leg(2, 2)
        down = lax.broadcasted_iota(jnp.int32, (rows, rows), 0)
        along = lax.broadcasted_iota(jnp.int32, (rows, rows), 1)
        diagonal = jnp.where(down == along, mask_ref[...].astype(jnp.float32), 0.0).astype(low_ref.dtype)
        low_ref[...] = jnp.dot(
            diagonal, cotangent_ref[...], preferred_element_type=jnp.float32
        ).astype(low_ref.dtype)
        projected_ref[...] = jnp.zeros_like(projected_ref)

    for index in range(last):

        @pl.when(block == index)
        def _(index=index):
            gather.arrive(index + 1)
            stored(index).start()

    branch_w = as_matrix(land_in[block])
    branch_ref[...] = jnp.dot(normed_ref[...], branch_w, preferred_element_type=jnp.float32)
    move_on(((0, ((3, 1), (2, 3))), (1, ((4, 2), (3, 3))), (2, ((4, 3),))))

    @pl.when(block == 0)
    def _():
        gather.arrive(0)
        share = land_small.shape[4]
        for z in range(land_small.shape[0]):
            for plane in range(land_small.shape[1]):
                owner = z * land_small.shape[1] + plane
                for side in range(2):
                    small_out[side * tall : (side + 1) * tall, owner * share : (owner + 1) * share] = land_small[
                        z, plane, side
                    ]

    small_ref = small_out.at[:, pl.ds(pl.multiple_of(block * width, width), width)]
    taps = small_rows(small_ref, *plan["taps"])
    shift = small_rows(small_ref, *plan["shift"])

    def some(index, at, carry):
        for tile in range(width // lanes):
            summed = conv_rows(index, at, 32, tile, branch_ref, offset_buf, taps, shift)
            sigma = sigmoid(summed)
            active = summed * sigma
            signal_ref[at, cut(tile)] = active.astype(signal_ref.dtype)
            slope_ref[at, cut(tile)] = sigma + active * (1.0 - sigma)
        return carry

    row_loop(rows, 32, some, 0)
    move_on(((0, ((4, 1), (3, 2))),))
    projected_ref[...] += contract(signal_ref[...], small_ref[:lanes, :], 1, 1)

    @pl.when(block == pl.num_programs(0) - 1)
    def _():
        high, low = high_low(projected_ref[...])
        own = own_tokens(rows)
        rank = plan["step"][1]
        size = plan["decay"][1]
        entry = lax.broadcasted_iota(jnp.int32, (lanes, lanes), 0)
        lane = lax.rem(lax.broadcasted_iota(jnp.int32, (lanes, lanes), 1), size)
        for first, pair in ((rank, write_pair), (rank + size, read_pair)):
            spread = (entry == lane + first).astype(jnp.bfloat16)
            parts = [
                (jnp.dot(part.astype(jnp.bfloat16), spread, preferred_element_type=jnp.float32) * own).reshape(
                    rows // chunk, chunk, lanes
                )
                for part in (high, low)
            ]
            pair[...] = jnp.concatenate(parts, axis=1).astype(pair.dtype)
        for index in range(last + 1):
            gather.drain(index)
        for index in range(2 * shares):
            rise.finish(index)
        for index in range(last):
            stored(index).wait()


def high_low(values):
    high = values.astype(jnp.bfloat16).astype(jnp.float32)
    return high, values - high


def own_tokens(rows):
    token = lax.rem(lax.broadcasted_iota(jnp.int32, (rows, lanes), 0), chunk)
    return (token == lax.div(lax.broadcasted_iota(jnp.int32, (rows, lanes), 1), lanes // chunk)).astype(
        jnp.float32
    )


def spread_all(pairs, target):
    some = 8

    def spread(index, carry):
        rows = jnp.concatenate([pairs[index * some + number] for number in range(some)], axis=1)
        wide = contract(rows, jnp.ones((rows.shape[0], lanes), rows.dtype), 0, 0)
        target[pl.ds(index * some * chunk, some * chunk)] = wide.reshape(some * chunk, -1, lanes)
        return carry

    lax.fori_loop(0, pairs.shape[0] // some, spread, 0)


def joined(first, second, hop):
    low = lax.bitwise_and(lax.broadcasted_iota(jnp.int32, first.shape, 0), hop) == 0
    return jnp.where(low, first, second) + pltpu.roll(jnp.where(low, second, first), hop, 0)


def folded(buffer, tile):
    parts = [buffer[tile, pl.ds(row * chunk, chunk), :] for row in range(chunk)]
    hop = 1
    while len(parts) > 1:
        parts = [joined(parts[index], parts[index + 1], hop) for index in range(0, len(parts), 2)]
        hop *= 2
    return parts[0]


def forward_kernel(
    plan,
    dims,
    lengths_ref,
    projected_ref,
    small_ref,
    signal_ref,
    write_pair,
    read_pair,
    gate_lines,
    out_lines,
    states_ref,
    step_ref,
    core_ref,
    begin_ref,
    gate_whole,
    out_whole,
    offset_buf,
    pre_buf,
    decay_step,
    flows,
    write_wide,
    read_wide,
    fold_a,
    fold_b,
    held_buf,
    *sems,
):
    rows, width = pre_buf.shape
    size = plan["decay"][1]
    half_size = size // 2
    tiles = width // lanes
    chunks = rows // chunk
    rank = plan["step"][1]
    group = pl.program_id(1)
    groups = pl.num_programs(1)
    moment = pl.program_id(0) * groups + group
    moments = pl.num_programs(0) * groups
    shares = gate_whole.shape[0]
    count = 2 * shares
    gather = Gather(
        dims,
        [lines.at[index] for index in range(shares) for lines in (gate_lines, out_lines)],
        [whole.at[index] for index in range(shares) for whole in (gate_whole, out_whole)],
        sems,
        [whole.shape[3:] for _ in range(shares) for whole in (gate_whole, out_whole)],
    )

    @pl.when(moment == 0)
    def _():
        Place(dims).greet()
        for which in range(count):
            gather.start(which)
        fill_offsets(lengths_ref, offset_buf, offset_buf.shape[0] - 8)
        spread_all(write_pair, write_wide)
        spread_all(read_pair, read_wide)

    @pl.when(group == 0)
    def _():
        held_buf[...] = jnp.zeros_like(held_buf)

    begin_ref[0] = held_buf[...]
    pre_buf[...] = jnp.dot(
        projected_ref[:, :rank].astype(small_ref.dtype),
        small_ref[pl.ds(plan["step"][0], rank), :],
        preferred_element_type=jnp.float32,
    )
    bias = small_rows(small_ref, *plan["bias"])

    def before(index, at, carry):
        spot = pl.ds(pl.multiple_of(index * 4, 4), 4)
        inside = offset_buf[pl.ds(pl.multiple_of(group * rows + index * 32, 32), 32), :] > 0
        for tile in range(tiles):
            step = softplus(pre_buf[at, cut(tile)] + bias[:, tile * lanes : (tile + 1) * lanes])
            step_ref[spot, :, cut(tile)] = step.reshape(4, chunk, lanes)
            decay_step[spot, :, cut(tile)] = jnp.where(inside, step, far).reshape(4, chunk, lanes)
            flow = step * signal_ref[at, cut(tile)].astype(jnp.float32)
            flows[spot, :, cut(tile)] = flow.reshape(4, chunk, lanes)
        return carry

    row_loop(rows, 4 * chunk, before, 0)
    rates = -jnp.exp(small_rows(small_ref, *plan["decay"])) * log2e
    rates = [rates[:, tile * lanes : (tile + 1) * lanes] for tile in range(tiles)]

    def advance(index, held, fold_buf):
        held = list(held)
        for place in range(chunk):
            now = index * chunk + place
            write_now = write_wide[group * rows + now]
            read_now = read_wide[group * rows + now]
            for tile in range(tiles):
                decay = jnp.exp2(rates[tile] * decay_step[index, pl.ds(place, 1), cut(tile)])
                fresh = decay * held[tile] + write_now * flows[index, pl.ds(place, 1), cut(tile)]
                held[tile] = fresh
                states_ref[now, :, cut(tile)] = fresh
                product = read_now * fresh
                fold_buf[tile, pl.ds(place * chunk, chunk), :] = product[:half_size] + product[half_size:]
        return tuple(held)

    def forward(pair, held):
        index = 2 * pair
        held = advance(index, held, fold_a)
        for tile in range(tiles):
            core_ref[index, :, cut(tile)] = folded(fold_a, tile)
        held = advance(index + 1, held, fold_b)
        for tile in range(tiles):
            core_ref[index + 1, :, cut(tile)] = folded(fold_b, tile)
        return held

    held = tuple(held_buf[:, cut(tile)] for tile in range(tiles))
    schedule = {}
    for which in range(count):
        for number in (2, 3):
            point = ((3, 5, 7, 10), (6, 8, 11, 14))[number - 2][which]
            schedule.setdefault(point, []).append((which, number))

    def move_on(legs):
        for which, number in legs:
            gather.leg(which, number)

    for half_loop in range(2):
        for point, legs in sorted(schedule.items()):
            if point < 16 and point % 2 == half_loop:
                pl.when(moment == point // 2)(functools.partial(move_on, legs))
        held = lax.fori_loop(half_loop * chunks // 4, (half_loop + 1) * chunks // 4, forward, held)
    for tile in range(tiles):
        held_buf[:, cut(tile)] = held[tile]

    @pl.when(moment == moments - 1)
    def _():
        for which in range(count):
            gather.arrive(which)
        for which in range(count):
            gather.drain(which)


def middle_kernel(
    plan,
    core_ref,
    small_ref,
    signal_ref,
    gate_w,
    low_ref,
    out_w,
    flipped_ref,
    normed_ref,
    tokens_ref,
    core_grad_ref,
    gate_grad_ref,
    skip_grad_ref,
    out_grad_ref,
    in_grad_ref,
    output_ref,
    pre_buf,
    gate_buf,
    gated_buf,
    out_buf,
    total,
):
    rows, width = pre_buf.shape
    tiles = width // lanes
    block = pl.program_id(0)
    each = out_w.shape[3]
    for index in range(out_w.shape[0]):
        out_buf[:, index * each : (index + 1) * each] = as_matrix(out_w[index][None])
    gate_buf[...] = jnp.dot(normed_ref[...], rows_of(gate_w), preferred_element_type=jnp.float32)
    pre_buf[...] = contract(low_ref[...], out_buf[...], 1, 1)
    skip = small_rows(small_ref, *plan["skip"])

    def after(index, at, carry):
        spot = pl.ds(pl.multiple_of(index * 4, 4), 4)
        sums = []
        for tile in range(tiles):
            signal = signal_ref[at, cut(tile)].astype(jnp.float32)
            core = core_ref[spot, :, cut(tile)].reshape(4 * chunk, lanes)
            core = core + skip[:, tile * lanes : (tile + 1) * lanes] * signal
            gate = gate_buf[at, cut(tile)]
            sigma = sigmoid(gate)
            active = gate * sigma
            gated_buf[at, cut(tile)] = (core * active).astype(gated_buf.dtype)
            grad_gated = pre_buf[at, cut(tile)]
            grad_core = grad_gated * active
            core_grad_ref[spot, :, cut(tile)] = grad_core.reshape(4, chunk, lanes)
            slope = sigma + active * (1.0 - sigma)
            gate_grad_ref[at, cut(tile)] = (grad_gated * core * slope).astype(gate_grad_ref.dtype)
            sums.append(carry[tile] + eight(grad_core * signal))
        return tuple(sums)

    zero_rows = jnp.zeros((8, lanes), jnp.float32)
    skips = row_loop(rows, 4 * chunk, after, (zero_rows,) * tiles)
    for tile in range(tiles):
        skip_grad_ref[:, cut(tile)] = jnp.sum(skips[tile], axis=0, keepdims=True)
    out_grad = contract(gated_buf[...], low_ref[...], 0, 0).astype(out_grad_ref.dtype)
    for index in range(out_w.shape[0]):
        out_grad_ref[index] = out_grad[:, index * each : (index + 1) * each]
    in_grad_ref[...] = jnp.dot(
        flipped_ref[...], gate_grad_ref[...], preferred_element_type=jnp.float32
    ).astype(in_grad_ref.dtype)
    piece = jnp.dot(gated_buf[...], out_buf[...], preferred_element_type=jnp.float32)

    @pl.when(block == 0)
    def _():
        total[...] = piece

    @pl.when(block > 0)
    def _():
        total[...] += piece

    @pl.when(block == pl.num_programs(0) - 1)
    def _():
        output_ref[...] = (tokens_ref[...].astype(jnp.float32) + total[...]).astype(output_ref.dtype)


def backward_kernel(
    plan,
    dims,
    lengths_ref,
    projected_ref,
    small_ref,
    signal_ref,
    write_pair,
    read_pair,
    step_ref,
    core_grad_ref,
    states_ref,
    begin_ref,
    out_grad_ref,
    in_grad_ref,
    signal_grad_ref,
    step_w_grad_ref,
    bias_grad_ref,
    decay_grad_ref,
    flat_ref,
    out_sum_ref,
    in_sum_ref,
    square_ref,
    offset_buf,
    decay_step,
    flows,
    write_wide,
    read_wide,
    first_a,
    first_b,
    second_a,
    second_b,
    through_buf,
    scaled_buf,
    low_buf,
    incoming_buf,
    rank_buf,
    write_buf,
    read_buf,
    *parts,
):
    rows, width = low_buf.shape
    rank = plan["step"][1]
    size = plan["decay"][1]
    half_size = size // 2
    tiles = width // lanes
    chunks = rows // chunk
    block = pl.program_id(0)
    turn = pl.program_id(1)
    groups = pl.num_programs(1)
    group = groups - 1 - turn
    moment = block * groups + turn
    moments = pl.num_programs(0) * groups
    gate_result, out_result, parts = parts[0], parts[1], parts[2:]
    pieces = gate_result.shape[0]
    count = 2 * pieces

    both = ((in_grad_ref, gate_result), (out_grad_ref, out_result))
    reduce = Reduce(
        dims,
        [ref.at[index] for index in range(pieces) for ref, _ in both],
        parts[: 6 * count],
        parts[6 * count :],
        [result.at[index] for index in range(pieces) for _, result in both],
        False,
    )

    @pl.when(moment == 0)
    def _():
        Place(dims).greet()
        for which in range(count):
            reduce.start(which)
        fill_offsets(lengths_ref, offset_buf, offset_buf.shape[0] - 8)
        spread_all(write_pair, write_wide)
        spread_all(read_pair, read_wide)
        write_buf[...] = jnp.zeros_like(write_buf)
        read_buf[...] = jnp.zeros_like(read_buf)
        rank_buf[...] = jnp.zeros_like(rank_buf)

    @pl.when(turn == 0)
    def _():
        incoming_buf[...] = jnp.zeros_like(incoming_buf)
        decay_grad_ref[...] = jnp.zeros_like(decay_grad_ref)
        bias_grad_ref[...] = jnp.zeros_like(bias_grad_ref)
        step_w_grad_ref[...] = jnp.zeros_like(step_w_grad_ref)

    def before(index, at, carry):
        spot = pl.ds(pl.multiple_of(index * 4, 4), 4)
        offsets = offset_buf[pl.ds(pl.multiple_of(group * rows + index * 32, 32), 32), :]
        inside = (offsets > 0).reshape(4, chunk, lanes)
        for tile in range(tiles):
            step = step_ref[spot, :, cut(tile)]
            decay_step[spot, :, cut(tile)] = jnp.where(inside, step, far)
            signal = signal_ref[at, cut(tile)].astype(jnp.float32).reshape(4, chunk, lanes)
            flows[spot, :, cut(tile)] = step * signal
        return carry

    row_loop(rows, 4 * chunk, before, 0)
    rates = -jnp.exp(small_rows(small_ref, *plan["decay"])) * log2e
    rates = [rates[:, tile * lanes : (tile + 1) * lanes] for tile in range(tiles)]

    def retreat(index, carried, first_buf, second_buf):
        incoming, decay_sums, current = (list(tiles_of) for tiles_of in carried)
        for place in range(chunk - 1, -1, -1):
            now = index * chunk + place
            token = group * rows + now
            write_now = write_wide[token]
            read_now = read_wide[token]
            read_sum = None
            write_sum = None
            for tile in range(tiles):
                grad_now = core_grad_ref[index, pl.ds(place, 1), cut(tile)]
                if place > 0:
                    earlier = states_ref[now - 1, :, cut(tile)]
                else:
                    earlier = jnp.where(
                        index > 0, states_ref[jnp.maximum(now - 1, 0), :, cut(tile)], begin_ref[0, :, cut(tile)]
                    )
                grad_state = incoming[tile] + read_now * grad_now
                through_read = current[tile] * grad_now
                current[tile] = earlier
                through_write = grad_state * flows[index, pl.ds(place, 1), cut(tile)]
                read_sum = through_read if read_sum is None else read_sum + through_read
                write_sum = through_write if write_sum is None else write_sum + through_write
                passed = grad_state * write_now
                first_buf[tile, pl.ds(place * chunk, chunk), :] = passed[:half_size] + passed[half_size:]
                exponent = rates[tile] * decay_step[index, pl.ds(place, 1), cut(tile)]
                leaving = jnp.exp2(exponent) * grad_state
                incoming[tile] = leaving
                weighted = (leaving * earlier) * exponent
                second_buf[tile, pl.ds(place * chunk, chunk), :] = weighted[:half_size] + weighted[half_size:]
                decay_sums[tile] = decay_sums[tile] + weighted
            read_buf[token] += read_sum
            write_buf[token] += write_sum
        return (tuple(incoming), tuple(decay_sums), tuple(current))

    def backward(pair, carried):
        index = chunks - 1 - 2 * pair
        for here, first_buf, second_buf in ((index, first_a, second_a), (index - 1, first_b, second_b)):
            carried = retreat(here, carried, first_buf, second_buf)
            for tile in range(tiles):
                through_buf[here, :, cut(tile)] = folded(first_buf, tile)
                scaled_buf[here, :, cut(tile)] = folded(second_buf, tile)
        return carried

    incoming = tuple(incoming_buf[:, cut(tile)] for tile in range(tiles))
    nothing = (jnp.zeros((size, lanes), jnp.float32),) * tiles
    current = tuple(states_ref[rows - 1, :, cut(tile)] for tile in range(tiles))
    schedule = {}
    for which in range(count):
        for number in (1, 2, 3):
            schedule.setdefault((2, 4, 7, 9)[which] + (0, 3, 5)[number - 1], []).append((which, number))

    def move_on(legs):
        for which, number in legs:
            reduce.leg(which, number)

    carried = (incoming, nothing, current)
    for half_loop in range(2):
        for point, legs in sorted(schedule.items()):
            if point % 2 == half_loop:
                pl.when(moment == point // 2)(functools.partial(move_on, legs))
        carried = lax.fori_loop(half_loop * chunks // 4, (half_loop + 1) * chunks // 4, backward, carried)
    incoming, decay_sums, _ = carried
    for tile in range(tiles):
        incoming_buf[:, cut(tile)] = incoming[tile]
        decay_grad_ref[:, cut(tile)] += decay_sums[tile] * ln2
    skip = small_rows(small_ref, *plan["skip"])

    def after(index, at, carry):
        spot = pl.ds(pl.multiple_of(index * 4, 4), 4)
        sums = []
        for tile in range(tiles):
            signal = signal_ref[at, cut(tile)].astype(jnp.float32)
            step = step_ref[spot, :, cut(tile)].reshape(4 * chunk, lanes)
            through = through_buf[spot, :, cut(tile)].reshape(4 * chunk, lanes)
            scaled = scaled_buf[spot, :, cut(tile)].reshape(4 * chunk, lanes)
            core_grad = core_grad_ref[spot, :, cut(tile)].reshape(4 * chunk, lanes)
            grad_pre = (through * signal + ln2 * scaled / jnp.maximum(step, tiny)) * slope_of(step)
            low_buf[at, cut(tile)] = grad_pre.astype(low_buf.dtype)
            signal_grad_ref[at, cut(tile)] = (
                through * step + skip[:, tile * lanes : (tile + 1) * lanes] * core_grad
            )
            sums.append(carry[tile] + eight(grad_pre))
        return tuple(sums)

    zero_rows = jnp.zeros((8, lanes), jnp.float32)
    sums = row_loop(rows, 4 * chunk, after, (zero_rows,) * tiles)
    for tile in range(tiles):
        bias_grad_ref[:, cut(tile)] += jnp.sum(sums[tile], axis=0, keepdims=True)
    step_w_grad_ref[...] += contract(
        projected_ref[:, :rank].astype(low_buf.dtype), low_buf[...], 0, 0
    )
    step_w = small_ref[pl.ds(plan["step"][0], rank), :]
    step_w = jnp.concatenate([step_w, jnp.zeros((lanes - rank, width), step_w.dtype)], axis=0)
    rank_buf[pl.ds(group * chunks, chunks)] += contract(low_buf[...], step_w, 1, 1).reshape(
        chunks, chunk, lanes
    )

    @pl.when(moment == moments - 1)
    def _():
        squares = jnp.zeros((8, lanes), jnp.float32)
        for which in range(count):
            squares = squares + reduce.finish(which)[0]
        square_ref[...] = squares
        some = 8
        entry = lax.rem(lax.broadcasted_iota(jnp.int32, (some * chunk * size, lanes), 0), size)
        target = lax.broadcasted_iota(jnp.int32, (some * chunk * size, lanes), 1)
        ones = jnp.ones((lanes, lanes), jnp.bfloat16)

        def lay(index, carry):
            lot = pl.ds(index * some * chunk, some * chunk)
            for number, buffer in enumerate((write_buf, read_buf)):
                high, low = high_low(buffer[lot].reshape(some * chunk * size, lanes))
                summed = jnp.dot(high.astype(jnp.bfloat16), ones, preferred_element_type=jnp.float32)
                summed += jnp.dot(low.astype(jnp.bfloat16), ones, preferred_element_type=jnp.float32)
                summed = jnp.where(target == entry + rank + number * size, summed, 0.0)
                summed = jnp.sum(summed.reshape(some * chunk, size, lanes), axis=1)
                rank_buf[pl.ds(index * some, some)] += summed.reshape(some, chunk, lanes)
            return carry

        lax.fori_loop(0, rank_buf.shape[0] // some, lay, 0)
        flat_ref[...] = rank_buf[...].reshape(flat_ref.shape).astype(flat_ref.dtype)
        for which in range(count):
            reduce.settle(which)
        for index in range(pieces):
            for target, result in ((out_sum_ref, out_result), (in_sum_ref, gate_result)):
                each = result.shape[2]
                target[:, index * each : (index + 1) * each] = result[index]


def back_kernel(
    plan,
    dims,
    lengths_ref,
    tokens_ref,
    low_ref,
    gain_ref,
    small_ref,
    flat_ref,
    branch_ref,
    signal_ref,
    slope_ref,
    signal_grad_ref,
    gate_grad_ref,
    flipped_ref,
    branch_w,
    gate_w,
    step_w_grad_ref,
    bias_grad_ref,
    decay_grad_ref,
    skip_grad_ref,
    plain_ref,
    earlier_ref,
    tokens_grad_ref,
    in_sum_ref,
    small_sum_ref,
    late_sum_ref,
    norm_ref,
    offset_buf,
    conv_buf,
    mixed_buf,
    total,
    in_stage,
    small_stage,
    late_stage,
    late_land,
    norm_own,
    norm_land,
    in_result,
    small_result,
    direct_send,
    direct_recv,
    *parts,
):
    rows = tokens_ref.shape[0]
    width = branch_ref.shape[1]
    tiles = width // lanes
    block = pl.program_id(0)
    last = in_stage.shape[0]
    count = last + 1
    reduce = Reduce(
        dims,
        [small_stage] + [in_stage.at[index] for index in range(last)],
        parts[: 5 * count],
        parts[5 * count :],
        [small_result] + [in_result.at[index] for index in range(last)],
        True,
    )
    share = small_stage.shape[4]
    half_rows = small_stage.shape[3]
    planes = small_stage.shape[1]
    owners = small_stage.shape[0] * planes

    @pl.when(block == 0)
    def _():
        Place(dims).greet(everyone=True)
        select_grad = contract(flat_ref[...], signal_ref[...], 0, 0)
        step_first, step_tall = plan["step"]
        filler = jnp.zeros((2 * half_rows - step_first - step_tall, select_grad.shape[1]), jnp.float32)
        pieces = {
            "decay": decay_grad_ref[...],
            "bias": bias_grad_ref[...],
            "skip": skip_grad_ref[...],
            "step": step_w_grad_ref[...],
        }
        first = plan["select"][1]
        rows_now = [select_grad[:first]]
        for name in ("decay", "taps", "shift", "bias", "skip", "gain"):
            tall = plan[name][1]
            rows_now.append(
                pieces[name] if name in pieces else jnp.zeros((tall, select_grad.shape[1]), jnp.float32)
            )
            first += tall
        rows_now.append(jnp.zeros((step_first - first, select_grad.shape[1]), jnp.float32))
        rows_now.append(pieces["step"])
        if filler.shape[0]:
            rows_now.append(filler)
        everything = jnp.concatenate(rows_now, axis=0)
        for owner in range(owners):
            for side in range(2):
                small_stage[owner // planes, owner % planes, side] = everything[
                    side * half_rows : (side + 1) * half_rows, owner * share : (owner + 1) * share
                ].astype(small_stage.dtype)
        reduce.start(0)
        fill_offsets(lengths_ref, offset_buf, rows)

    def move_on(plan_of_moves):
        for moment, legs in plan_of_moves:

            @pl.when(block == moment)
            def _(legs=legs):
                for which, number in legs:
                    reduce.leg(which, number)

    taps = small_rows(small_ref, *plan["taps"])
    taps_count = taps.shape[0]
    zero_rows = jnp.zeros((8, lanes), jnp.float32)

    @pl.when(block < last)
    def _():
        conv_buf[pl.ds(0, rows), :] = signal_grad_ref[...] + jnp.dot(
            flat_ref[...], small_ref[:lanes, :], preferred_element_type=jnp.float32
        )
        conv_buf[pl.ds(rows, 8), :] = jnp.zeros((8, width), jnp.float32)

        def through_conv(index, at, carry):
            sums = []
            for tile in range(tiles):
                grad_conv = conv_buf[at, cut(tile)] * slope_ref[at, cut(tile)]
                conv_buf[at, cut(tile)] = grad_conv
                sums.append(carry[tile] + eight(grad_conv))
            return tuple(sums)

        shift_sums = row_loop(rows, 32, through_conv, (zero_rows,) * tiles)
        move_on(((0, ((0, 1),)), (1, ((1, 1), (0, 3))), (2, ((2, 1), (1, 3))), (3, ((3, 1), (2, 3)))))

        def to_branch(index, at, carry):
            longer = pl.ds(pl.multiple_of(index * 32, 32), 40)
            offsets = offset_buf[longer, :]
            result = []
            for tile in range(tiles):
                here = slice(tile * lanes, (tile + 1) * lanes)
                grads = conv_buf[longer, cut(tile)]
                branch = branch_ref[at, cut(tile)]
                summed = taps[taps_count - 1 : taps_count, here] * grads[:32]
                sums = [None] * taps_count
                sums[taps_count - 1] = carry[tile][taps_count - 1] + eight(branch * grads[:32])
                for tap in range(taps_count - 1):
                    lag = taps_count - 1 - tap
                    moved = pltpu.roll(jnp.where(offsets >= lag, grads, 0.0), 40 - lag, 0)[:32]
                    summed = summed + taps[tap : tap + 1, here] * moved
                    sums[tap] = carry[tile][tap] + eight(branch * moved)
                mixed_buf[block, at, cut(tile)] = summed.astype(mixed_buf.dtype)
                result.append(tuple(sums))
            return tuple(result)

        sums = row_loop(rows, 32, to_branch, ((zero_rows,) * taps_count,) * tiles)
        in_grad = jnp.dot(flipped_ref[...], mixed_buf[block], preferred_element_type=jnp.float32)
        in_stage[block] = in_grad.reshape(in_stage.shape[1:]).astype(in_stage.dtype)
        for index in range(last):

            @pl.when(block == index)
            def _(index=index):
                reduce.start(index + 1)

        late = [
            jnp.concatenate(
                [jnp.sum(sums[tile][tap], axis=0, keepdims=True) for tap in range(taps_count)]
                + [jnp.sum(shift_sums[tile], axis=0, keepdims=True)]
                + [jnp.zeros((8 - taps_count - 1, lanes), jnp.float32)],
                axis=0,
            )
            for tile in range(tiles)
        ]
        late = jnp.concatenate(late, axis=1)
        for piece in range(width // share):
            late_stage[block * (width // share) + piece] = late[:, piece * share : (piece + 1) * share]
        move_on(((0, ((0, 2),)), (1, ((1, 2),)), (2, ((2, 2),)), (3, ((3, 2),))))

    @pl.when(block >= last)
    def _():
        grad_normed_piece = contract(mixed_buf[block - last], rows_of(branch_w), 1, 1)
        grad_normed_piece += contract(gate_grad_ref[...], rows_of(gate_w), 1, 1)

        @pl.when(block == last)
        def _():
            total[...] = grad_normed_piece

        @pl.when(block > last)
        def _():
            total[...] += grad_normed_piece

        move_on(((4, ((4, 1), (3, 3))), (6, ((4, 2),)), (7, ((4, 3),))))

    @pl.when(block == pl.num_programs(0) - 1)
    def _():
        def finish(index, at, carry):
            residual = tokens_ref[at, :].astype(jnp.float32)
            scale = lax.rsqrt(jnp.mean(residual * residual, axis=1, keepdims=True) + epsilon)
            grad_normed = total[at, :]
            weighted = grad_normed * gain_ref[...]
            inner = jnp.mean(weighted * residual, axis=1, keepdims=True)
            grad_y = low_ref[at, :].astype(jnp.float32)
            result = grad_y + (scale * weighted - residual * (scale * scale * scale) * inner)
            tokens_grad_ref[at, :] = result.astype(tokens_grad_ref.dtype)
            return carry + eight(grad_normed * residual * scale)

        gains = row_loop(rows, 16, finish, jnp.zeros((8, total.shape[1]), jnp.float32))
        gains = jnp.sum(gains, axis=0, keepdims=True)
        place = Place(dims)
        each = gains.shape[1] // owners
        for owner in range(owners):
            late_stage[owner, taps_count + 1 : taps_count + 2, :each] = gains[
                :, owner * each : (owner + 1) * each
            ]
        late_sems = direct_send.at[0], direct_recv.at[0]
        norm_sems = direct_send.at[1], direct_recv.at[1]
        send_to_everyone(place, lambda chip: late_stage.at[chip], late_land, *late_sems)
        more, plain = reduce.finish(0, plain_ref)
        kept = earlier_ref[...] + more
        for index in range(1, count - 1):
            kept = kept + reduce.finish(index)[0]
        late_sum = sum_of_everyone(place, late_stage[place.me], late_land, *late_sems)
        late_sum_ref[...] = late_sum
        kept = kept + folded_squares(late_sum * late_sum) * (1 - place.core).astype(jnp.float32)
        kept = kept + reduce.finish(count - 1)[0]
        norm_own[...] = jnp.stack([kept, plain])
        send_to_everyone(place, lambda chip: norm_own, norm_land, *norm_sems)
        norm_ref[...] = sum_of_everyone(place, norm_own[...], norm_land, *norm_sems)
        for index in range(count):
            reduce.settle(index)
        for index in range(last):
            in_sum_ref[:, index * width : (index + 1) * width] = in_result[index]
        small_sum_ref[...] = small_result[...]


def finish_kernel(
    plan, names, late, tokens_ref, branch_ref, gate_ref, out_ref, small_ref, late_ref, norm_ref, *outs
):
    middle = branch_ref.shape[1]
    outs[0][:, :middle] = branch_ref[...]
    outs[0][:, middle:] = gate_ref[...]
    outs[1][...] = out_ref[...]
    outs[2][...] = tokens_ref[...]
    for name, target in zip(names, outs[3 : 3 + len(names)]):
        source, (first, count) = (late_ref, late[name]) if name in late else (small_ref, plan[name])
        if len(target.shape) == 1:
            target[...] = source[first, : target.shape[0]]
        else:
            target[...] = source[first : first + count, :]
    for index in range(2):
        outs[3 + len(names) + index][0, 0] = jnp.sum(norm_ref[index])


def shape(dims, kind=jnp.float32):
    return jax.ShapeDtypeStruct(dims, kind)


def compute_call(
    kernel, name, blocks, in_specs, out_specs, out_shape, scratch, flops, operands, collective_id=None
):
    return pl.pallas_call(
        kernel,
        grid=blocks if isinstance(blocks, tuple) else (blocks,),
        in_specs=in_specs,
        out_specs=out_specs,
        out_shape=out_shape,
        scratch_shapes=scratch,
        compiler_params=pltpu.CompilerParams(
            dimension_semantics=("arbitrary",) * (len(blocks) if isinstance(blocks, tuple) else 1),
            vmem_limit_bytes=62 * 1024 * 1024,
            collective_id=collective_id,
            has_side_effects=collective_id is not None,
        ),
        cost_estimate=pl.CostEstimate(flops=flops, bytes_accessed=40 << 20, transcendentals=0),
        name=name,
    )(*operands)


class Place:
    def __init__(self, dims, swapped=False):
        depth, tall, wide = dims
        self.dims = dims
        self.core = lax.axis_index("wide")
        self.me = lax.axis_index("narrow")
        self.across = lax.rem(self.me, wide)
        self.up = lax.rem(lax.div(self.me, wide), tall)
        self.deep = lax.div(self.me, wide * tall)
        side = 1 - self.core if swapped else self.core
        turn = side if tall == wide else 0
        self.second = (1 + turn * (wide - 1), self.across + turn * (self.up - self.across), wide)
        self.third = (wide - turn * (wide - 1), self.up + turn * (self.across - self.up), tall)
        self.spans = (depth, wide, tall)
        self.other = {"wide": 1 - self.core}

    def level(self, d):
        return lax.rem(self.deep + d, self.spans[0])

    def plane(self, e, f):
        return (
            lax.rem(self.second[1] + e, self.second[2]) * self.second[0]
            + lax.rem(self.third[1] + f, self.third[2]) * self.third[0]
        )

    def plane_behind(self, e, f):
        return self.plane((self.spans[1] - e) % self.spans[1], (self.spans[2] - f) % self.spans[2])

    def at(self, d, e, f):
        return {"narrow": self.level(d) * (self.dims[1] * self.dims[2]) + self.plane(e, f)}

    def greet(self, everyone=False):
        barrier = pltpu.get_barrier_semaphore()
        peers = [self.other]
        if everyone:
            number = self.spans[0] * self.spans[1] * self.spans[2]
            for hop in range(1, number):
                chip = lax.rem(self.me + hop, number)
                peers += [{"narrow": chip}, {"wide": 1 - self.core, "narrow": chip}]
        else:
            for axis, size in enumerate(self.spans):
                for hop in range(1, size):
                    move = [0, 0, 0]
                    move[axis] = hop
                    peers.append(self.at(*move))
        for peer in peers:
            pl.semaphore_signal(barrier, inc=1, device_id=peer, device_id_type=pl.DeviceIdType.MESH)
        pl.semaphore_wait(barrier, len(peers))


def by_rows(block):
    return block[0] % 32 == 0


def half_shape(block):
    if len(block) == 3:
        return tuple(block[1:])
    return (block[0] // 2, block[1]) if by_rows(block) else (block[0], block[1] // 2)


def half(view, block, side, lead=0):
    ahead = (slice(None),) * lead
    if len(block) == 3:
        return view.at[ahead + (side,)]
    if by_rows(block):
        return view.at[ahead + (pl.ds(pl.multiple_of(side * (block[0] // 2), 16), block[0] // 2),)]
    columns = pl.ds(pl.multiple_of(side * (block[1] // 2), lanes), block[1] // 2)
    return view.at[ahead + (slice(None), columns)]


def remote(source, target, send_sem, recv_sem, device):
    return pltpu.make_async_remote_copy(
        src_ref=source,
        dst_ref=target,
        send_sem=send_sem,
        recv_sem=recv_sem,
        device_id=device,
        device_id_type=pl.DeviceIdType.MESH,
    )


class Gather:
    def __init__(self, dims, own, whole, sems, blocks=None):
        self.dims, self.own, self.whole = dims, own, whole
        self.local_sem, self.send_sem, self.recv_sem = sems
        self.lined = blocks is not None
        self.blocks = blocks or [block.shape for block in own]

    @staticmethod
    def sems(count, dims):
        copies = dims[0] + 2 * dims[1] * dims[2]
        return [pltpu.SemaphoreType.DMA((count,))] + [pltpu.SemaphoreType.DMA((count, copies))] * 2

    def line(self, which, plane, side):
        return half(self.whole[which].at[:, plane], self.blocks[which], side, 1)

    def local(self, place, which):
        block = self.blocks[which]
        if self.lined:
            return pltpu.make_async_copy(
                self.own[which], self.line(which, place.plane(0, 0), place.core), self.local_sem.at[which]
            )
        return pltpu.make_async_copy(
            half(self.own[which], block, place.core),
            half(self.whole[which].at[place.deep, place.plane(0, 0)], block, place.core),
            self.local_sem.at[which],
        )

    def copy(self, which, source, target, index, device):
        return remote(
            source, target, self.send_sem.at[which, index], self.recv_sem.at[which, index], device
        )

    def rise(self, place, which, hop):
        block = self.blocks[which]
        return self.copy(
            which,
            half(self.own[which], block, place.core),
            half(self.whole[which].at[place.deep, place.plane(0, 0)], block, place.core),
            hop,
            place.at(hop, 0, 0),
        )

    def leg_index(self, e, f):
        return self.dims[0] + e * self.dims[1] + f

    def hand_index(self, e, f):
        return self.leg_index(e, f) + self.dims[1] * self.dims[2]

    def onward(self, place, which, e, f):
        line = self.line(which, place.plane_behind(e, f), place.core)
        source = self.own[which] if self.lined and e == 0 and f == 0 else line
        if f == 0:
            for hop in range(1, place.spans[2]):
                self.copy(which, source, line, self.leg_index(e, hop), place.at(0, 0, hop)).start()
        if f == 0 and e == 0:
            for hop in range(1, place.spans[1]):
                self.copy(which, source, line, self.leg_index(hop, 0), place.at(0, hop, 0)).start()
        self.copy(which, source, line, self.hand_index(e, f), place.other).start()

    def start(self, which):
        place = Place(self.dims)
        if self.lined:
            self.onward(place, which, 0, 0)
            self.local(place, which).start()
            return
        for hop in range(1, place.spans[0]):
            self.rise(place, which, hop).start()
        self.local(place, which).start()

    def leg(self, which, number):
        place = Place(self.dims)
        if number == 1:
            self.local(place, which).wait()
            for hop in range(1, place.spans[0]):
                self.rise(place, which, hop).wait_recv()
            self.onward(place, which, 0, 0)
            return
        for e in range(place.spans[1]):
            for f in range(place.spans[2]):
                if (number == 2 and f == 0 and e > 0) or (number == 3 and f > 0):
                    line = self.line(which, place.plane_behind(e, f), place.core)
                    self.copy(which, line, line, self.leg_index(e, f), place.other).wait_recv()
                    self.onward(place, which, e, f)

    def arrive(self, which):
        place, mirror = Place(self.dims), Place(self.dims, swapped=True)
        for e in range(place.spans[1]):
            for f in range(place.spans[2]):
                line = self.line(which, mirror.plane_behind(e, f), 1 - place.core)
                self.copy(which, line, line, self.hand_index(e, f), place.other).wait_recv()

    def drain(self, which):
        place = Place(self.dims)
        if self.lined:
            self.local(place, which).wait()
        else:
            for hop in range(1, place.spans[0]):
                self.rise(place, which, hop).wait_send()
        for e in range(place.spans[1]):
            for f in range(place.spans[2]):
                line = self.line(which, place.plane_behind(e, f), place.core)
                if e > 0 or f > 0:
                    self.copy(which, line, line, self.leg_index(e, f), place.other).wait_send()
                self.copy(which, line, line, self.hand_index(e, f), place.other).wait_send()


class Rise:
    def __init__(self, dims, own, lines, sems):
        self.dims, self.own, self.lines = dims, own, lines
        self.local_sem, self.send_sem, self.recv_sem = sems

    @staticmethod
    def sems(count, dims):
        return [pltpu.SemaphoreType.DMA((count,))] + [pltpu.SemaphoreType.DMA((count, dims[0]))] * 2

    def copies(self, place, which):
        source = half(self.own[which], self.own[which].shape, place.core)
        target = self.lines[which].at[place.deep]
        local = pltpu.make_async_copy(source, target, self.local_sem.at[which])
        return local, [
            remote(
                source, target, self.send_sem.at[which, hop], self.recv_sem.at[which, hop], place.at(hop, 0, 0)
            )
            for hop in range(1, place.spans[0])
        ]

    def start(self, which):
        local, sends = self.copies(Place(self.dims), which)
        for copy in [*sends, local]:
            copy.start()

    def finish(self, which):
        local, sends = self.copies(Place(self.dims), which)
        local.wait()
        for copy in sends:
            copy.wait_recv()
            copy.wait_send()


class Reduce:
    def __init__(self, dims, grads, rooms, sems, results, resident):
        self.dims, self.grads, self.resident = dims, grads, resident
        count = len(grads)
        self.mine, self.swapped, self.third, self.second, self.first = (
            rooms[index * count : (index + 1) * count] for index in range(5)
        )
        self.loaded = None if resident else rooms[5 * count :]
        self.load_sem, self.swap_send, self.swap_recv, self.send_sem, self.recv_sem = sems[:5]
        self.last_send, self.last_recv = sems[5:]
        self.results = results

    @staticmethod
    def rooms(dims, grads, resident):
        depth, tall, wide = dims
        leads = (
            (tall, wide, depth),
            (depth, tall * wide),
            (tall - 1, wide, depth),
            (wide - 1, depth),
            (depth - 1,),
        )
        if not resident:
            leads += ((depth, tall * wide),)
        return [
            pltpu.VMEM(lead + half_shape(grad.shape[2:]), grad.dtype) for lead in leads for grad in grads
        ]

    @staticmethod
    def sems(count, dims):
        return (
            [pltpu.SemaphoreType.DMA((count,))] * 3
            + [pltpu.SemaphoreType.DMA((count, dims[0] + dims[1] + dims[2]))] * 2
            + [pltpu.SemaphoreType.DMA((count,))] * 2
        )

    def block(self, which):
        return self.grads[which].shape[2:]

    def load(self, place, which):
        return pltpu.make_async_copy(
            half(self.grads[which], self.block(which), place.core, 2),
            self.loaded[which],
            self.load_sem.at[which],
        )

    def swap(self, place, which):
        return remote(
            half(self.grads[which], self.block(which), 1 - place.core, 2),
            self.swapped[which],
            self.swap_send.at[which],
            self.swap_recv.at[which],
            place.other,
        )

    def hop(self, which, source, target, index, device):
        return remote(
            source, target, self.send_sem.at[which, index], self.recv_sem.at[which, index], device
        )

    def third_hop(self, place, which, f):
        return self.hop(which, self.mine[which].at[f], self.third[which].at[f - 1], f, place.at(0, 0, f))

    def second_hop(self, place, which, e):
        return self.hop(
            which,
            self.mine[which].at[0, e],
            self.second[which].at[e - 1],
            self.dims[1] + e,
            place.at(0, e, 0),
        )

    def first_hop(self, place, which, d):
        return self.hop(
            which,
            self.mine[which].at[0, 0, place.level(d)],
            self.first[which].at[d - 1],
            self.dims[1] + self.dims[2] + d,
            place.at(d, 0, 0),
        )

    def start(self, which):
        place = Place(self.dims)
        self.swap(place, which).start()
        if not self.resident:
            self.load(place, which).start()

    def parts(self, place, which, e, f, z):
        plane = place.plane(e, f)
        if self.resident:
            found = [half(self.grads[which].at[z, plane], self.block(which), place.core)]
        else:
            found = [self.loaded[which].at[z, plane]]
        found.append(self.swapped[which].at[z, plane])
        if f == 0:
            found += [self.third[which].at[hop - 1, e, z] for hop in range(1, place.spans[2])]
        if f == 0 and e == 0:
            found += [self.second[which].at[hop - 1, z] for hop in range(1, place.spans[1])]
        return found

    def ready(self, place, which):
        if not self.resident:
            self.load(place, which).wait()
        self.swap(place, which).wait_recv()

    def added(self, parts, store, carry):
        rows = parts[0].shape[0]
        group = min(rows, 16)

        def some(index, carry):
            at_rows = pl.ds(pl.multiple_of(index * group, group), group)
            total = parts[0][at_rows, :].astype(jnp.float32)
            for part in parts[1:]:
                total = total + part[at_rows, :].astype(jnp.float32)
            return store(at_rows, total, carry)

        return lax.fori_loop(0, rows // group, some, carry)

    def sum_into(self, place, which, e, f, z):
        target = self.mine[which].at[f, e, z]

        def keep(at_rows, total, carry):
            target[at_rows, :] = total.astype(target.dtype)
            return carry

        self.added(self.parts(place, which, e, f, z), keep, 0)

    def leg(self, which, number):
        place = Place(self.dims)
        depth, span_e, span_f = place.spans
        if number == 1:
            self.ready(place, which)
            for f in range(span_f - 1, 0, -1):
                for e in range(span_e - 1, -1, -1):
                    for z in range(depth):
                        self.sum_into(place, which, e, f, z)
                self.third_hop(place, which, f).start()
        elif number == 2:
            for f in range(1, span_f):
                self.third_hop(place, which, f).wait_recv()
            for e in range(span_e - 1, 0, -1):
                for z in range(depth):
                    self.sum_into(place, which, e, 0, z)
                self.second_hop(place, which, e).start()
        else:
            if span_e == 1:
                for f in range(1, span_f):
                    self.third_hop(place, which, f).wait_recv()
            for e in range(1, span_e):
                self.second_hop(place, which, e).wait_recv()
            for d in range(1, depth):
                self.sum_into(place, which, 0, 0, place.level(d))
                self.first_hop(place, which, d).start()

    def result(self, which, side):
        return half(self.results[which], self.block(which), side)

    def last(self, place, which, side):
        share = self.result(which, side)
        return remote(share, share, self.last_send.at[which], self.last_recv.at[which], place.other)

    def finish(self, which, marks=None):
        place = Place(self.dims)
        parts = self.parts(place, which, 0, 0, place.deep)
        for d in range(1, place.spans[0]):
            self.first_hop(place, which, d).wait_recv()
            parts.append(self.first[which].at[d - 1])
        share = self.result(which, place.core)

        def store(at_rows, total, carry):
            share[at_rows, :] = total
            kept, plain = carry
            squared = total * total
            if marks is not None:
                marked = squared * marks[place.core, at_rows, :]
                plain = plain + folded_squares(marked)
                squared = squared - marked
            return (kept + folded_squares(squared), plain)

        squares = self.added(parts, store, (jnp.zeros((8, lanes), jnp.float32),) * 2)
        self.last(place, which, place.core).start()
        return squares

    def settle(self, which):
        place = Place(self.dims)
        last = self.last(place, which, 1 - place.core)
        last.wait_recv()
        last.wait_send()
        self.swap(place, which).wait_send()
        for f in range(1, place.spans[2]):
            self.third_hop(place, which, f).wait_send()
        for e in range(1, place.spans[1]):
            self.second_hop(place, which, e).wait_send()
        for d in range(1, place.spans[0]):
            self.first_hop(place, which, d).wait_send()


def folded_squares(values):
    total = None
    if values.shape[1] < lanes:
        first = lax.broadcasted_iota(jnp.int32, (values.shape[0], lanes), 1) == 0
        values = jnp.where(first, jnp.sum(values, axis=1, keepdims=True), 0.0)
    for row in range(0, values.shape[0], 8):
        for column in range(0, values.shape[1], lanes):
            piece = values[row : row + 8, column : column + lanes]
            total = piece if total is None else total + piece
    return total


def send_to_all(place, source, landing, send_sem, recv_sem):
    number = landing.shape[0]
    for hop in range(1, number):
        target = lax.rem(place.me + hop, number)
        remote(
            source(target), landing.at[place.me], send_sem.at[hop], recv_sem.at[hop], {"narrow": target}
        ).start()


def wait_for_all(place, own, landing, send_sem, recv_sem):
    number = landing.shape[0]
    landing[place.me] = own
    for hop in range(1, number):
        came = landing.at[lax.rem(place.me + number - hop, number)]
        copy = remote(came, came, send_sem.at[hop], recv_sem.at[hop], place.other)
        copy.wait_recv()
        copy.wait_send()


def send_to_everyone(place, source, landing, send_sem, recv_sem):
    number = landing.shape[1]
    target = landing.at[place.core, place.me]

    def send(hop, carry):
        chip = lax.rem(place.me + hop, number)
        for turn in range(2):
            device = {"wide": lax.rem(place.core + turn, 2), "narrow": chip}
            remote(source(chip), target, send_sem.at[turn, hop], recv_sem.at[turn, hop], device).start()
        return carry

    lax.fori_loop(1, number, send, 0)
    remote(source(place.me), target, send_sem.at[1, 0], recv_sem.at[1, 0], place.other).start()


def sum_of_everyone(place, own, landing, send_sem, recv_sem):
    number = landing.shape[1]
    landing[place.core, place.me] = own

    def wait(turn, hop):
        came = landing.at[lax.rem(place.core + turn, 2), lax.rem(place.me + number - hop, number)]
        copy = remote(came, came, send_sem.at[turn, hop], recv_sem.at[turn, hop], place.other)
        copy.wait_recv()
        copy.wait_send()

    def wait_both(hop, carry):
        wait(0, hop)
        wait(1, hop)
        return carry

    lax.fori_loop(1, number, wait_both, 0)
    wait(1, 0)

    def add(spot, total):
        return total + landing[0, spot] + landing[1, spot]

    return lax.fori_loop(1, number, add, landing[0, 0] + landing[1, 0])


def grid_of(mesh):
    number = mesh.shape["narrow"]
    places = [getattr(device, "coords", None) for device in mesh.devices[0]]
    if all(place is not None for place in places):
        sizes = [len({place[axis] for place in places}) for axis in (2, 1, 0)]
        if sizes[0] * sizes[1] * sizes[2] == number:
            return tuple(sizes)
    side = round((number / 2) ** (1 / 3))
    return (2 * side, side, side) if 2 * side**3 == number else (number, 1, 1)


def plan_of(select_rows, state_size, tap_count, step_rows):
    plan, first = {}, 0
    for name, tall in (
        ("select", select_rows),
        ("decay", state_size),
        ("taps", tap_count),
        ("shift", 1),
        ("bias", 1),
        ("skip", 1),
        ("gain", 1),
    ):
        plan[name] = (first, tall)
        first += tall
    plan["step"] = (lanes, step_rows)
    plan["rows"] = -(-(lanes + step_rows) // 32) * 32
    return plan


def per_device(
    dims,
    tokens,
    cotangent,
    loss_mask,
    seq_lengths,
    norm_gain,
    in_proj,
    conv_weight,
    conv_bias,
    select_proj,
    step_proj,
    step_bias,
    decay_log,
    skip_scale,
    out_proj,
):
    half = jnp.bfloat16
    piece = skip_scale.shape[0]
    gain_piece = norm_gain.shape[0]
    rank, size = step_proj.shape[0], decay_log.shape[0]
    plan = plan_of(select_proj.shape[0], size, conv_weight.shape[0], rank)
    smalls = {
        "select": select_proj,
        "decay": decay_log,
        "taps": conv_weight,
        "shift": conv_bias[None],
        "bias": step_bias[None],
        "skip": skip_scale[None],
        "gain": norm_gain[None],
        "step": step_proj,
    }
    depth, planes = dims[0], dims[1] * dims[2]
    number = depth * planes
    in_rows = in_proj.shape[0]
    rows, model = tokens.shape
    inner = piece * number
    width = 4 * lanes
    blocks = inner // width
    chunks = rows // chunk
    mask_row = loss_mask[None]

    whole = pl.BlockSpec(memory_space=pltpu.VMEM)
    tall = pl.BlockSpec((rows, width), lambda b: (0, b))
    deep = pl.BlockSpec((chunks, chunk, width), lambda b: (0, 0, b))
    lead = pl.BlockSpec((rows, size, width), lambda b: (0, 0, b))
    first_w = pl.BlockSpec((model, width), lambda b: (0, b))
    second_w = pl.BlockSpec((model, width), lambda b: (0, b + blocks))
    out_w = pl.BlockSpec((width, model), lambda b: (b, 0))

    def thin(height):
        return pl.BlockSpec((height, width), lambda b: (0, b))

    def fixed(*dims_of):
        return pl.BlockSpec(dims_of, lambda b: (0,) * len(dims_of))

    scalars = pl.BlockSpec(memory_space=pltpu.SMEM)
    offset_buf = pltpu.VMEM((rows + 8, lanes), jnp.int32)
    packed = thin(plan["rows"])

    pair = (chunks, 2 * chunk, lanes)
    pair = (chunks, 2 * chunk, lanes)
    anywhere = pl.BlockSpec(memory_space=pl.ANY)
    small_half = (2, plan["rows"] // 2, piece)
    in_piece = (in_rows, width)
    shares = 2
    in_share = (in_rows, inner // shares)
    out_share = (out_proj.shape[0], model // shares)
    lines = [shape((shares, depth) + half_shape(block), half) for block in (in_share, out_share)]
    (
        branch,
        signal,
        slope,
        projected,
        flipped,
        normed,
        grad_low,
        write_pair,
        read_pair,
        small,
        gain_value,
        in_blocks,
        gate_lines,
        out_lines,
    ) = compute_call(
        functools.partial(front_kernel, plan, dims, tuple(smalls)),
        "front",
        blocks,
        [scalars, whole, whole, whole] + [whole] * len(smalls) + [whole] * 2,
        [tall, tall, tall] + [whole] * 8 + [anywhere] * 3,
        [
            shape((rows, inner)),
            shape((rows, inner), half),
            shape((rows, inner)),
            shape((rows, lanes)),
            shape((model, rows), half),
            shape((rows, model), half),
            shape((rows, model), half),
            shape(pair, half),
            shape(pair, half),
            shape((plan["rows"], inner), half),
            shape((1, model)),
            shape((blocks, depth, planes) + in_piece, half),
            *lines,
        ],
        [
            offset_buf,
            pltpu.VMEM((plan["rows"], piece), jnp.float32),
            pltpu.VMEM(small_half, half),
            pltpu.VMEM((blocks,) + in_piece, half),
            pltpu.VMEM((shares,) + in_share, half),
            pltpu.VMEM((shares,) + out_share, half),
            pltpu.VMEM((depth, planes) + small_half, half),
            pltpu.VMEM((blocks, depth, planes) + in_piece, half),
            pltpu.SemaphoreType.DMA((blocks,)),
            pltpu.VMEM((8, piece), jnp.float32),
            pltpu.VMEM((number, 8, piece), jnp.float32),
            pltpu.SemaphoreType.DMA((number,)),
            pltpu.SemaphoreType.DMA((number,)),
        ]
        + Gather.sems(1 + blocks, dims)
        + Rise.sems(2 * shares, dims),
        4 * rows * model * inner,
        (seq_lengths, tokens, cotangent, mask_row, *smalls.values(), in_proj, out_proj),
        collective_id=0,
    )
    groups = 2
    part, pieces = rows // groups, chunks // groups
    row_block = pltpu.VMEM((pieces, chunk, width), jnp.float32)
    spread_block = pltpu.VMEM((rows, size, lanes), jnp.float32)
    fold_block = pltpu.VMEM((width // lanes, chunk * chunk, lanes), jnp.float32)

    def by_group(order, *dims_of):
        middle = (0,) * (len(dims_of) - 2)
        return pl.BlockSpec(dims_of, lambda b, g: (order(g),) + middle + (b,))

    def by_token(order, *dims_of):
        return pl.BlockSpec(dims_of, lambda b, g: (order(g),) + (0,) * (len(dims_of) - 1))

    def by_channel(height):
        return pl.BlockSpec((height, width), lambda b, g: (0, b))

    def onward(g):
        return g

    def backward(g):
        return groups - 1 - g

    states, step, core, begins, gate_blocks, out_blocks = compute_call(
        functools.partial(forward_kernel, plan, dims),
        "forward",
        (blocks, groups),
        [
            scalars,
            by_token(onward, part, lanes),
            by_channel(plan["rows"]),
            by_group(onward, part, width),
            whole,
            whole,
            anywhere,
            anywhere,
        ],
        [
            by_group(onward, part, size, width),
            by_group(onward, pieces, chunk, width),
            by_group(onward, pieces, chunk, width),
            by_group(onward, 1, size, width),
            anywhere,
            anywhere,
        ],
        [
            shape((rows, size, inner)),
            shape((chunks, chunk, inner)),
            shape((chunks, chunk, inner)),
            shape((groups, size, inner)),
            shape((shares, depth, planes) + in_share, half),
            shape((shares, depth, planes) + out_share, half),
        ],
        [
            offset_buf,
            pltpu.VMEM((part, width), jnp.float32),
            row_block,
            row_block,
            spread_block,
            spread_block,
            fold_block,
            fold_block,
            pltpu.VMEM((size, width), jnp.float32),
        ]
        + Gather.sems(2 * shares, dims),
        15 * rows * inner * size,
        (seq_lengths, projected, small, signal, write_pair, read_pair, gate_lines, out_lines),
        collective_id=2,
    )
    split = in_share[1] // width
    weights = pl.BlockSpec((None, number, in_rows, width), lambda b: (b // split, 0, 0, b % split))
    per_block = width // out_share[0]
    out_pieces = pl.BlockSpec((shares, per_block) + out_share, lambda b: (0, b, 0, 0))
    branch_whole = in_blocks.reshape(blocks, number, *in_piece)
    gate_whole = gate_blocks.reshape(shares, number, *in_share)
    out_whole = out_blocks.reshape(shares, number, *out_share)
    core_grad, gate_grad, grad_skip, grad_outw, grad_in_gate, output = compute_call(
        functools.partial(middle_kernel, plan),
        "middle",
        blocks,
        [deep, packed, tall, weights, whole, out_pieces, whole, whole, whole],
        [
            deep,
            tall,
            thin(1),
            pl.BlockSpec((shares, width, out_share[1]), lambda b: (0, b, 0)),
            pl.BlockSpec((None, model, width), lambda b: (b // split, 0, b % split)),
            fixed(rows, model),
        ],
        [
            shape((chunks, chunk, inner)),
            shape((rows, inner), half),
            shape((1, inner)),
            shape((shares, inner, out_share[1]), half),
            shape((shares, model, in_share[1]), half),
            shape((rows, model), half),
        ],
        [
            pltpu.VMEM((rows, width), jnp.float32),
            pltpu.VMEM((rows, width), jnp.float32),
            pltpu.VMEM((rows, width), half),
            pltpu.VMEM((width, model), half),
            pltpu.VMEM((rows, model), jnp.float32),
        ],
        8 * rows * model * inner,
        (core, small, signal, gate_whole, grad_low, out_whole, flipped, normed, tokens),
    )
    early_grads = [
        grad_outw.reshape((shares, depth, planes) + out_share),
        grad_in_gate.reshape((shares, depth, planes) + in_share),
    ]
    early_sums = [shape(out_proj.shape), shape((in_rows, inner))]
    early_pieces = [shape((depth, planes) + block, half) for block in (in_share, out_share)] * shares
    (
        signal_grad,
        grad_stepw,
        grad_bias,
        grad_decaylog,
        flat,
        out_sum,
        in_gate_sum,
        early_squares,
    ) = compute_call(
        functools.partial(backward_kernel, plan, dims),
        "backward",
        (blocks, groups),
        [
            scalars,
            by_token(backward, part, lanes),
            by_channel(plan["rows"]),
            by_group(backward, part, width),
            whole,
            whole,
            by_group(backward, pieces, chunk, width),
            by_group(backward, pieces, chunk, width),
            by_group(backward, part, size, width),
            by_group(backward, 1, size, width),
            anywhere,
            anywhere,
        ],
        [
            by_group(backward, part, width),
            by_channel(rank),
            by_channel(1),
            by_channel(size),
            whole,
        ]
        + [whole] * 3,
        [
            shape((rows, inner)),
            shape((rank, inner)),
            shape((1, inner)),
            shape((size, inner)),
            shape((rows, lanes), half),
            *early_sums,
            shape((8, lanes)),
        ],
        [
            offset_buf,
            row_block,
            row_block,
            spread_block,
            spread_block,
            fold_block,
            fold_block,
            fold_block,
            fold_block,
            row_block,
            row_block,
            pltpu.VMEM((part, width), half),
            pltpu.VMEM((size, width), jnp.float32),
            pltpu.VMEM((chunks, chunk, lanes), jnp.float32),
            spread_block,
            spread_block,
        ]
        + [pltpu.VMEM((shares,) + block, jnp.float32) for block in (in_share, out_share)]
        + Reduce.rooms(dims, early_pieces, False)
        + Reduce.sems(2 * shares, dims),
        40 * rows * inner * size,
        (
            seq_lengths,
            projected,
            small,
            signal,
            write_pair,
            read_pair,
            step,
            core_grad,
            states,
            begins,
            *early_grads,
        ),
        collective_id=3,
    )

    plain_rows = np.zeros((plan["rows"], piece), np.float32)
    for name in ("bias", "decay", "skip"):
        first, count = plan[name]
        plain_rows[first : first + count] = 1.0
    late_grads = [shape((depth, planes) + small_half, half)]
    late_grads += [shape((depth, planes, in_rows, width), half)] * blocks
    taps_n = conv_weight.shape[0]
    late = {"taps": (0, taps_n), "shift": (taps_n, 1), "gain": (taps_n + 1, 1)}
    late_block = (8, piece)

    early_tall = pl.BlockSpec((rows, width), lambda b: (0, jnp.minimum(b, blocks - 1)))
    late_tall = pl.BlockSpec((rows, width), lambda b: (0, jnp.maximum(b - blocks, 0)))
    tokens_grad, in_branch_sum, small_sum, late_sum, norms = compute_call(
        functools.partial(back_kernel, plan, dims),
        "back",
        2 * blocks,
        [scalars, whole, whole, whole]
        + [pl.BlockSpec((plan["rows"], width), lambda b: (0, jnp.minimum(b, blocks - 1))), whole]
        + [early_tall, whole, early_tall, early_tall, late_tall, whole]
        + [
            pl.BlockSpec((None, number, in_rows, width), lambda b: (jnp.maximum(b - blocks, 0), 0, 0, 0)),
            pl.BlockSpec(
                (None, number, in_rows, width),
                lambda b: (jnp.maximum(b - blocks, 0) // split, 0, 0, jnp.maximum(b - blocks, 0) % split),
            ),
        ]
        + [whole] * 6,
        [whole] * 5,
        [
            shape((rows, model), half),
            shape((in_rows, inner)),
            shape(small_half),
            shape(late_block),
            shape((2, 8, lanes)),
        ],
        [
            offset_buf,
            pltpu.VMEM((rows + 8, width), jnp.float32),
            pltpu.VMEM((blocks, rows, width), half),
            pltpu.VMEM((rows, model), jnp.float32),
            pltpu.VMEM((blocks,) + late_grads[1].shape, half),
            pltpu.VMEM(late_grads[0].shape, late_grads[0].dtype),
            pltpu.VMEM((number,) + late_block, jnp.float32),
            pltpu.VMEM((2, number) + late_block, jnp.float32),
            pltpu.VMEM((2, 8, lanes), jnp.float32),
            pltpu.VMEM((2, number, 2, 8, lanes), jnp.float32),
            pltpu.VMEM((blocks, in_rows, width), jnp.float32),
            pltpu.VMEM(small_half, jnp.float32),
            pltpu.SemaphoreType.DMA((2, 2, number)),
            pltpu.SemaphoreType.DMA((2, 2, number)),
        ]
        + Reduce.rooms(dims, late_grads, True)
        + Reduce.sems(blocks + 1, dims),
        8 * rows * model * inner,
        (
            seq_lengths,
            tokens,
            grad_low,
            gain_value,
            small,
            flat,
            branch,
            signal,
            slope,
            signal_grad,
            gate_grad,
            flipped,
            branch_whole,
            gate_whole,
            grad_stepw,
            grad_bias,
            grad_decaylog,
            grad_skip,
            jnp.asarray(plain_rows.reshape(small_half)),
            early_squares,
        ),
        collective_id=1,
    )

    names = ("gain", "taps", "shift", "select", "step", "bias", "decay", "skip")
    own = (norm_gain, conv_weight, conv_bias, select_proj, step_proj, step_bias, decay_log, skip_scale)
    in_grad, out_grad, grad_tokens, gain_grad, *small_grads, decay_sq, plain_sq = pl.pallas_call(
        functools.partial(finish_kernel, plan, names, late),
        in_specs=[whole] * 7,
        out_specs=[whole] * (3 + len(names)) + [scalars] * 2,
        out_shape=[shape(in_proj.shape), shape(out_proj.shape), shape(tokens.shape, half)]
        + [shape(array.shape) for array in own]
        + [shape((1, 1))] * 2,
        name="finish",
    )(
        tokens_grad,
        in_branch_sum,
        in_gate_sum,
        out_sum,
        small_sum.reshape(plan["rows"], piece),
        late_sum,
        norms,
    )
    return (
        output,
        grad_tokens,
        gain_grad,
        in_grad,
        *small_grads,
        out_grad,
        decay_sq[0, 0],
        plain_sq[0, 0],
    )


def solution(mesh):
    placed = (
        P(("wide", "narrow"), None),
        P(("wide", "narrow"), None),
        P(("wide", "narrow")),
        P(("wide", "narrow"), None),
        P("narrow"),
        P("narrow", None),
        P(None, "narrow"),
        P("narrow"),
        P(None, "narrow"),
        P(None, "narrow"),
        P("narrow"),
        P(None, "narrow"),
        P("narrow"),
        P("narrow", None),
    )
    return jax.shard_map(
        functools.partial(per_device, grid_of(mesh)),
        mesh=mesh,
        in_specs=placed,
        out_specs=(
            P(("wide", "narrow"), None),
            P(("wide", "narrow"), None),
            P("narrow"),
            P("narrow", None),
            P(None, "narrow"),
            P("narrow"),
            P(None, "narrow"),
            P(None, "narrow"),
            P("narrow"),
            P(None, "narrow"),
            P("narrow"),
            P("narrow", None),
            P(),
            P(),
        ),
        check_vma=False,
    )
```

profile of v0, /device:TPU:0, one launch (start us, length us, event | category | flops | bytes accessed | tf_op | source)
XLA Modules:
  0.0 273.5 jit_solution(10354262085432104529)
XLA Ops:
  0.6 53.2 %front.1 = (f32[512,2048]{1,0:T(8,128)}, bf16[512,2048]{1,0:T(8,128)(2,1)}, f32[512,2048]{1,0:T(8,128)}, f32[512,128]{1,0:T(8,128)}, bf16[1024,512]{1,0:T(8,128)...) custom-call(s32[1,3]{1,0:T(1,128)} %lengths_ref.7, ...), custom_call_target="tpu_custom_call" | custom-call | flops 4294967296 | bytes 41943040 | tf_op jit(solution)/shard_map/front/pallas_call | solution.py:1001
  53.8 51.7 %forward.1 = (f32[512,16,2048]{2,1,0:T(8,128)}, f32[64,8,2048]{2,1,0:T(8,128)}, f32[64,8,2048]{2,1,0:T(8,128)}, f32[2,16,2048]{2,1,0:T(8,128)}, bf16[2,4,4,64,10...) custom-call(s32[1,3]{1,0:T(1,128)} %lengths_ref.7, f32[512,128]{1,0:T(8,128)} %get-tuple-element.66.projected_ref, ...), custom_call_target="tpu_custom_call" | custom-call | flops 251658240 | bytes 41943040 | tf_op jit(solution)/shard_map/forward/pallas_call | solution.py:1001
  105.5 22.2 %middle.1 = (f32[64,8,2048]{2,1,0:T(8,128)}, bf16[512,2048]{1,0:T(8,128)(2,1)}, f32[1,2048]{1,0:T(1,128)}, bf16[2,2048,512]{2,1,0:T(8,128)(2,1)}, bf16[2,1024,10...) custom-call(f32[64,8,2048]{2,1,0:T(8,128)} %get-tuple-element.73.core_ref, bf16[192,2048]{1,0:T(8,128)(2,1)} %get-tuple-element.67.small_ref, ...), custom_call_target="tpu_custom_call" | custom-call | flops 8589934592 | bytes 41943040 | tf_op jit(solution)/shard_map/middle/pallas_call | solution.py:1001
  127.7 76.8 %backward.1 = (f32[512,2048]{1,0:T(8,128)}, f32[64,2048]{1,0:T(8,128)}, f32[1,2048]{1,0:T(1,128)}, f32[16,2048]{1,0:T(8,128)}, bf16[512,128]{1,0:T(8,128)(2,1)},...) custom-call(s32[1,3]{1,0:T(1,128)} %lengths_ref.7, f32[512,128]{1,0:T(8,128)} %get-tuple-element.66.projected_ref, ...), custom_call_target="tpu_custom_call" | custom-call | flops 671088640 | bytes 41943040 | tf_op jit(solution)/shard_map/backward/pallas_call | solution.py:1001
  204.5 65.4 %back.1 = (bf16[512,1024]{1,0:T(8,128)(2,1)}, f32[64,2048]{1,0:T(8,128)}, f32[2,96,128]{2,1,0:T(8,128)}, f32[8,128]{1,0:T(8,128)}, f32[2,8,128]{2,1,0:T(8,128)}) custom-call(s32[1,3]{1,0:T(1,128)} %lengths_ref.7, bf16[512,1024]{1,0:T(8,128)(2,1)} %tokens_ref.5, bf16[512,1024]{1,0:T(8,128)(2,1)} %get-tuple-element.75.low_ref, ...), custom_call_target="tpu_custom_call" | custom-call | flops 8589934592 | bytes 41943040 | tf_op jit(solution)/shard_map/back/pallas_call | solution.py:1001
  270.0 3.3 %finish.1 = (f32[64,4096]{1,0:T(8,128)}, f32[128,1024]{1,0:T(8,128)}, bf16[512,1024]{1,0:T(8,128)(2,1)}, f32[64]{0:T(128)}, f32[4,128]{1,0:T(4,128)}, /*index=5*...) custom-call(bf16[512,1024]{1,0:T(8,128)(2,1)} %get-tuple-element.98., ...), custom_call_target="tpu_custom_call" | custom-call | tf_op jit(solution)/shard_map/finish/pallas_call | solution.py:1936
where the time goes:
time: 274 us; the launch traced here: 273 us
  Pallas kernels  273 us (100%)
    pallas_call x5, Pallas kernels, compute_call(): pl.pallas_call(kernel, grid=blocks if isinstance(blocks, tuple) else (blo...  269 us

commit v1 on v0

--- a/solution.py
+++ b/solution.py
@@ -166,8 +166,6 @@
             own_gate[index] = in_ref[:, first + index * each : first + (index + 1) * each].astype(own_gate.dtype)
             each = own_out.shape[2]
             own_out[index] = out_ref[:, index * each : (index + 1) * each].astype(own_out.dtype)
-        for index in range(2 * shares):
-            rise.start(index)
         fill_offsets(lengths_ref, offset_buf, rows)
         gather.leg(1, 1)
         gather.leg(0, 1)
@@ -188,6 +186,7 @@
         gather.leg(1, 2)
         gather.leg(0, 2)
         gather.leg(2, 1)
+        rise.start(0)
         flipped_ref[...] = normed_ref[...].T
         gather.leg(1, 3)
         gather.leg(0, 3)
@@ -210,6 +209,7 @@
     branch_w = as_matrix(land_in[block])
     branch_ref[...] = jnp.dot(normed_ref[...], branch_w, preferred_element_type=jnp.float32)
     move_on(((0, ((3, 1), (2, 3))), (1, ((4, 2), (3, 3))), (2, ((4, 3),))))
+    pl.when(block == 0)(functools.partial(rise.start, 1))
 
     @pl.when(block == 0)
     def _():
@@ -238,6 +238,12 @@
 
     row_loop(rows, 32, some, 0)
     move_on(((0, ((4, 1), (3, 2))),))
+
+    @pl.when(block == 0)
+    def _():
+        for index in range(2, 2 * shares):
+            rise.start(index)
+
     projected_ref[...] += contract(signal_ref[...], small_ref[:lanes, :], 1, 1)
 
     @pl.when(block == pl.num_programs(0) - 1)
@@ -813,34 +819,6 @@
     @pl.when(block == 0)
     def _():
         Place(dims).greet(everyone=True)
-        select_grad = contract(flat_ref[...], signal_ref[...], 0, 0)
-        step_first, step_tall = plan["step"]
-        filler = jnp.zeros((2 * half_rows - step_first - step_tall, select_grad.shape[1]), jnp.float32)
-        pieces = {
-            "decay": decay_grad_ref[...],
-            "bias": bias_grad_ref[...],
-            "skip": skip_grad_ref[...],
-            "step": step_w_grad_ref[...],
-        }
-        first = plan["select"][1]
-        rows_now = [select_grad[:first]]
-        for name in ("decay", "taps", "shift", "bias", "skip", "gain"):
-            tall = plan[name][1]
-            rows_now.append(
-                pieces[name] if name in pieces else jnp.zeros((tall, select_grad.shape[1]), jnp.float32)
-            )
-            first += tall
-        rows_now.append(jnp.zeros((step_first - first, select_grad.shape[1]), jnp.float32))
-        rows_now.append(pieces["step"])
-        if filler.shape[0]:
-            rows_now.append(filler)
-        everything = jnp.concatenate(rows_now, axis=0)
-        for owner in range(owners):
-            for side in range(2):
-                small_stage[owner // planes, owner % planes, side] = everything[
-                    side * half_rows : (side + 1) * half_rows, owner * share : (owner + 1) * share
-                ].astype(small_stage.dtype)
-        reduce.start(0)
         fill_offsets(lengths_ref, offset_buf, rows)
 
     def move_on(plan_of_moves):
@@ -871,8 +849,6 @@
             return tuple(sums)
 
         shift_sums = row_loop(rows, 32, through_conv, (zero_rows,) * tiles)
-        move_on(((0, ((0, 1),)), (1, ((1, 1), (0, 3))), (2, ((2, 1), (1, 3))), (3, ((3, 1), (2, 3)))))
-
         def to_branch(index, at, carry):
             longer = pl.ds(pl.multiple_of(index * 32, 32), 40)
             offsets = offset_buf[longer, :]
@@ -914,7 +890,44 @@
         late = jnp.concatenate(late, axis=1)
         for piece in range(width // share):
             late_stage[block * (width // share) + piece] = late[:, piece * share : (piece + 1) * share]
-        move_on(((0, ((0, 2),)), (1, ((1, 2),)), (2, ((2, 2),)), (3, ((3, 2),))))
+        move_on(
+            (
+                (1, ((1, 1), (0, 1))),
+                (2, ((2, 1), (1, 2), (0, 2))),
+                (3, ((3, 1), (2, 2), (1, 3), (0, 3))),
+            )
+        )
+
+        @pl.when(block == 0)
+        def _():
+            select_grad = contract(flat_ref[...], signal_ref[...], 0, 0)
+            step_first, step_tall = plan["step"]
+            filler = jnp.zeros((2 * half_rows - step_first - step_tall, select_grad.shape[1]), jnp.float32)
+            pieces = {
+                "decay": decay_grad_ref[...],
+                "bias": bias_grad_ref[...],
+                "skip": skip_grad_ref[...],
+                "step": step_w_grad_ref[...],
+            }
+            first = plan["select"][1]
+            rows_now = [select_grad[:first]]
+            for name in ("decay", "taps", "shift", "bias", "skip", "gain"):
+                tall = plan[name][1]
+                rows_now.append(
+                    pieces[name] if name in pieces else jnp.zeros((tall, select_grad.shape[1]), jnp.float32)
+                )
+                first += tall
+            rows_now.append(jnp.zeros((step_first - first, select_grad.shape[1]), jnp.float32))
+            rows_now.append(pieces["step"])
+            if filler.shape[0]:
+                rows_now.append(filler)
+            everything = jnp.concatenate(rows_now, axis=0)
+            for owner in range(owners):
+                for side in range(2):
+                    small_stage[owner // planes, owner % planes, side] = everything[
+                        side * half_rows : (side + 1) * half_rows, owner * share : (owner + 1) * share
+                    ].astype(small_stage.dtype)
+            reduce.start(0)
 
     @pl.when(block >= last)
     def _():
@@ -929,7 +942,7 @@
         def _():
             total[...] += grad_normed_piece
 
-        move_on(((4, ((4, 1), (3, 3))), (6, ((4, 2),)), (7, ((4, 3),))))
+        move_on(((4, ((3, 2),)), (5, ((4, 1), (2, 3))), (6, ((3, 3),)), (7, ((4, 2),))))
 
     @pl.when(block == pl.num_programs(0) - 1)
     def _():
@@ -955,6 +968,7 @@
         late_sems = direct_send.at[0], direct_recv.at[0]
         norm_sems = direct_send.at[1], direct_recv.at[1]
         send_to_everyone(place, lambda chip: late_stage.at[chip], late_land, *late_sems)
+        reduce.leg(4, 3)
         more, plain = reduce.finish(0, plain_ref)
         kept = earlier_ref[...] + more
         for index in range(1, count - 1):

time: 274 us -> 269 us (0.982)
  Pallas kernels: 273 us -> 267 us
    pallas_call x5, Pallas kernels: 269 us -> 264 us  [compute_call(): pl.pallas_call(kernel, grid=blocks if isinstance(blocks, tuple) else (blo...]
where the time goes in v1:
time: 269 us; the launch traced here: 268 us
  Pallas kernels  267 us (99%)
    pallas_call x5, Pallas kernels, compute_call(): pl.pallas_call(kernel, grid=blocks if isinstance(blocks, tuple) else (blo...  264 us

profile of v1, /device:TPU:0, one launch (start us, length us, event | category | flops | bytes accessed | tf_op | source)
XLA Modules:
  0.0 267.7 jit_solution(5477336770700299409)
XLA Ops:
  0.6 52.8 %front.1 = (f32[512,2048]{1,0:T(8,128)}, bf16[512,2048]{1,0:T(8,128)(2,1)}, f32[512,2048]{1,0:T(8,128)}, f32[512,128]{1,0:T(8,128)}, bf16[1024,512]{1,0:T(8,128)...) custom-call(s32[1,3]{1,0:T(1,128)} %lengths_ref.7, ...), custom_call_target="tpu_custom_call" | custom-call | flops 4294967296 | bytes 41943040 | tf_op jit(solution)/shard_map/front/pallas_call | solution.py:1015
  53.5 52.6 %forward.1 = (f32[512,16,2048]{2,1,0:T(8,128)}, f32[64,8,2048]{2,1,0:T(8,128)}, f32[64,8,2048]{2,1,0:T(8,128)}, f32[2,16,2048]{2,1,0:T(8,128)}, bf16[2,4,4,64,10...) custom-call(s32[1,3]{1,0:T(1,128)} %lengths_ref.7, f32[512,128]{1,0:T(8,128)} %get-tuple-element.66.projected_ref, ...), custom_call_target="tpu_custom_call" | custom-call | flops 251658240 | bytes 41943040 | tf_op jit(solution)/shard_map/forward/pallas_call | solution.py:1015
  106.1 22.2 %middle.1 = (f32[64,8,2048]{2,1,0:T(8,128)}, bf16[512,2048]{1,0:T(8,128)(2,1)}, f32[1,2048]{1,0:T(1,128)}, bf16[2,2048,512]{2,1,0:T(8,128)(2,1)}, bf16[2,1024,10...) custom-call(f32[64,8,2048]{2,1,0:T(8,128)} %get-tuple-element.73.core_ref, bf16[192,2048]{1,0:T(8,128)(2,1)} %get-tuple-element.67.small_ref, ...), custom_call_target="tpu_custom_call" | custom-call | flops 8589934592 | bytes 41943040 | tf_op jit(solution)/shard_map/middle/pallas_call | solution.py:1015
  128.3 76.7 %backward.1 = (f32[512,2048]{1,0:T(8,128)}, f32[64,2048]{1,0:T(8,128)}, f32[1,2048]{1,0:T(1,128)}, f32[16,2048]{1,0:T(8,128)}, bf16[512,128]{1,0:T(8,128)(2,1)},...) custom-call(s32[1,3]{1,0:T(1,128)} %lengths_ref.7, f32[512,128]{1,0:T(8,128)} %get-tuple-element.66.projected_ref, ...), custom_call_target="tpu_custom_call" | custom-call | flops 671088640 | bytes 41943040 | tf_op jit(solution)/shard_map/backward/pallas_call | solution.py:1015
  205.0 59.2 %back.1 = (bf16[512,1024]{1,0:T(8,128)(2,1)}, f32[64,2048]{1,0:T(8,128)}, f32[2,96,128]{2,1,0:T(8,128)}, f32[8,128]{1,0:T(8,128)}, f32[2,8,128]{2,1,0:T(8,128)}) custom-call(s32[1,3]{1,0:T(1,128)} %lengths_ref.7, bf16[512,1024]{1,0:T(8,128)(2,1)} %tokens_ref.5, bf16[512,1024]{1,0:T(8,128)(2,1)} %get-tuple-element.75.low_ref, ...), custom_call_target="tpu_custom_call" | custom-call | flops 8589934592 | bytes 41943040 | tf_op jit(solution)/shard_map/back/pallas_call | solution.py:1015
  264.2 3.3 %finish.1 = (f32[64,4096]{1,0:T(8,128)}, f32[128,1024]{1,0:T(8,128)}, bf16[512,1024]{1,0:T(8,128)(2,1)}, f32[64]{0:T(128)}, f32[4,128]{1,0:T(4,128)}, /*index=5*...) custom-call(bf16[512,1024]{1,0:T(8,128)(2,1)} %get-tuple-element.98., ...), custom_call_target="tpu_custom_call" | custom-call | tf_op jit(solution)/shard_map/finish/pallas_call | solution.py:1950
